TPU v7x, 32 devices: a whole 2x2x4 slice. The times are simulated.
32 devices in a mesh: dp: 32 (over z, y, x, core).
Axes of the slice: x: 2, y: 2, z: 4, core: 2. Of those that a mesh axis runs over, the one named last changes fastest.
Arguments:
- block_in: bfloat16 [32, 1024, 1024], P('dp'), may hold values from -6 to 6
- condition: float32 [32, 1024], P('dp'), may hold values from -6 to 6
- out_grad: bfloat16 [32, 1024, 1024], P('dp'), may hold values from -6 to 6
- weights: float32 [1024, 18432], P('dp'), may hold values from -2 to 2, as said below
- biases: float32 [14336], P('dp'), may hold values from -0.75 to 0.75
- first_moment: float32 [1024, 18432], P('dp'), may hold values from -32 to 32
- second_moment: float32 [1024, 18432], P('dp'), may hold values from 131.072 to 983.04
- bias_first: float32 [14336], P('dp'), may hold values from -32 to 32
- bias_second: float32 [14336], P('dp'), may hold values from 131.072 to 983.04
Outputs:
- block_out: bfloat16 [32, 1024, 1024], P('dp')
- input_grad: float32 [32, 1024, 1024], P('dp')
- condition_grad: float32 [32, 1024], P('dp')
- weight_grad: float32 [1024, 18432], P('dp')
- bias_grad: float32 [14336], P('dp')
- new_weights: float32 [1024, 18432], P('dp')
- new_biases: float32 [14336], P('dp')
- new_first: float32 [1024, 18432], P('dp')
- new_second: float32 [1024, 18432], P('dp')
- new_bias_first: float32 [14336], P('dp')
- new_bias_second: float32 [14336], P('dp')
Inputs may be any that keep to these rules, and one draw needn't show every extreme that they name: `weights`: columns as described in the first step.
All inputs are finite; a program needn't handle non-finite values.
Results may differ from a plain program's by a relative error of at most 0.017.
The roundings to bfloat16 on the way count: a program that leaves them out, or rounds other values in their place, can miss the bound.
Values may be sent and summed in bfloat16 or wider, within the bound.
A program may use at most 320 MiB of HBM per device.

v0:
```python
import functools

import jax
import jax.numpy as jnp
from jax import lax
from jax.experimental import pallas as pl
from jax.experimental.pallas import tpu as pltpu
from jax.sharding import PartitionSpec as P

D = 1024
FF = 4096
S = 1024
STEP = 3
CH = 512
NJ = FF // CH
VMEM_BYTES = 64 * 2**20
STEPS = 8
learn_rate = 0.01
beta_first = 0.9
beta_second = 0.95
adam_eps = 1e-08
weight_decay = 0.05
gc = 0.7978845608028654
LOG2E = 1.4426950408889634
f32 = jnp.float32
bf = jnp.bfloat16
NT = (((1,), (1,)), ((), ()))
TN = (((0,), (0,)), ((), ()))
V = pl.BlockSpec(memory_space=pltpu.VMEM)
A = pl.BlockSpec(memory_space=pl.ANY)
sd = jax.ShapeDtypeStruct
MESH = pl.DeviceIdType.MESH


def mesh_signal(sem, dev):
    pl.semaphore_signal(sem, inc=1, device_id=(dev,), device_id_type=MESH)


def remote(src, dst, send, recv, dev):
    return pltpu.make_async_remote_copy(src_ref=src, dst_ref=dst, send_sem=send, recv_sem=recv, device_id=(dev,), device_id_type=MESH)


def greet_all(n, me, between):
    barrier = pltpu.get_barrier_semaphore()

    def go(k, _):
        mesh_signal(barrier, lax.rem(me + k, n))
        return 0

    lax.fori_loop(1, n, go, 0)
    between()
    pl.semaphore_wait(barrier, n - 1)


def each_peer(n, me, f):
    def go(k, _):
        f(k, lax.rem(me + k, n), lax.rem(me + n - k, n))
        return 0

    lax.fori_loop(1, n, go, 0)


def gather_sems(count):
    return [pltpu.SemaphoreType.DMA((count,)), pltpu.SemaphoreType.DMA((count, 12)), pltpu.SemaphoreType.DMA((count, 12))]


def each_mate(n, me, f):
    def go(k, _):
        f(k, lax.rem(me + 2 * k, n), lax.rem(me + n - 2 * k, n))
        return 0

    lax.fori_loop(1, n // 2, go, 0)


class Place:
    def __init__(self):
        me = lax.axis_index("dp")
        self.me = me
        self.z = me // 8
        self.y = lax.rem(me // 4, 2)
        self.x = lax.rem(me // 2, 2)
        self.c = lax.rem(me, 2)
        self.to_c = me + 1 - 2 * self.c
        self.to_x = me + 2 - 4 * self.x
        self.to_y = me + 4 - 8 * self.y
        self.a = self.z // 2
        self.b = lax.rem(self.z, 2)
        self.to_b = me + 8 - 16 * self.b
        self.to_a = me + 16 - 32 * self.a

    def to_z(self, k):
        return lax.rem(self.z + k, 4) * 8 + lax.rem(self.me, 8)


class Gather:
    def __init__(self, at, src, buf, local, send, recv, count):
        self.at, self.src, self.buf, self.local, self.send, self.recv, self.count = at, src, buf, local, send, recv, count

    def step_refs(self, i, step, c):
        at, b = self.at, self.buf.at[i]
        y, x = at.y, at.x
        lo, hi = pl.ds(0, 16), pl.ds(16, 16)
        if step == 1:
            return [b.at[:, y, x, c]]
        if step == 2:
            return [b.at[:, y, 1 - x, c, lo], b.at[:, 1 - y, x, c, hi]]
        return [b.at[:, 1 - y, :, c, lo], b.at[:, :, 1 - x, c, hi]]

    def z_copy(self, i, k):
        at = self.at
        return remote(self.src.at[i], self.buf.at[i, at.z, at.y, at.x, at.c], self.send.at[i, k - 1], self.recv.at[i, k - 1], at.to_z(k))

    def z_landed(self, i, k):
        at = self.at
        zz = lax.rem(at.z + 4 - k, 4)
        return remote(self.src.at[i], self.buf.at[i, zz, at.y, at.x, at.c], self.send.at[i, k - 1], self.recv.at[i, k - 1], at.to_z(k))

    def own(self, i):
        at = self.at
        return pltpu.make_async_copy(self.src.at[i], self.buf.at[i, at.z, at.y, at.x, at.c], self.local.at[i])

    def xy_copies(self, i, step):
        at, b = self.at, self.buf.at[i]
        y, x, c = at.y, at.x, at.c
        lo, hi = pl.ds(0, 16), pl.ds(16, 16)
        if step == 2:
            a, d = b.at[:, y, x, c, lo], b.at[:, y, x, c, hi]
            return [
                remote(a, a, self.send.at[i, 3], self.recv.at[i, 3], at.to_x),
                remote(d, d, self.send.at[i, 4], self.recv.at[i, 4], at.to_y),
            ]
        a, d = b.at[:, y, :, c, lo], b.at[:, :, x, c, hi]
        return [
            remote(a, a, self.send.at[i, 5], self.recv.at[i, 5], at.to_y),
            remote(d, d, self.send.at[i, 6], self.recv.at[i, 6], at.to_x),
        ]

    def xy_landed(self, i, step):
        at, b = self.at, self.buf.at[i]
        refs = self.step_refs(i, step, at.c)
        base = 3 if step == 2 else 5
        return [remote(r, r, self.send.at[i, base + q], self.recv.at[i, base + q], at.to_x) for q, r in enumerate(refs)]

    def core_copies(self, i, step):
        at = self.at
        base = {1: 7, 2: 8, 3: 10}[step]
        return [remote(r, r, self.send.at[i, base + q], self.recv.at[i, base + q], at.to_c) for q, r in enumerate(self.step_refs(i, step, at.c))]

    def core_landed(self, i, step):
        at = self.at
        base = {1: 7, 2: 8, 3: 10}[step]
        return [remote(r, r, self.send.at[i, base + q], self.recv.at[i, base + q], at.to_c) for q, r in enumerate(self.step_refs(i, step, 1 - at.c))]

    def start(self, first, last):
        def go(i, _):
            self.own(i).start()
            return 0

        lax.fori_loop(first, last, go, 0)

    def tick(self, t, parts=(5, 4, 3, 2, 1)):
        def one():
            for k in (1, 2, 3):
                self.z_copy(t, k).start()

        def two():
            i = t - 1
            for k in (1, 2, 3):
                self.z_landed(i, k).wait_recv()
            self.own(i).wait()
            for cp in self.xy_copies(i, 2) + self.core_copies(i, 1):
                cp.start()

        def three():
            i = t - 2
            for cp in self.xy_landed(i, 2):
                cp.wait_recv()
            for cp in self.xy_copies(i, 3) + self.core_copies(i, 2):
                cp.start()

        def four():
            i = t - 3
            for cp in self.xy_landed(i, 3):
                cp.wait_recv()
            for cp in self.core_copies(i, 3):
                cp.start()

        def five():
            i = t - 4
            for step in (1, 2, 3):
                for cp in self.core_landed(i, step):
                    cp.wait_recv()

        for part in parts:
            i = t - part + 1
            when((i >= 0) & (i < self.count), (one, two, three, four, five)[part - 1])

    def finish(self):
        def go(i, _):
            for k in (1, 2, 3):
                self.z_copy(i, k).wait_send()
            for step in (2, 3):
                for cp in self.xy_copies(i, step):
                    cp.wait_send()
            for step in (1, 2, 3):
                for cp in self.core_copies(i, step):
                    cp.wait_send()
            return 0

        lax.fori_loop(0, self.count, go, 0)


def dot(a,b,dn=None):
    if dn is None: return jnp.dot(a,b,preferred_element_type=f32)
    return lax.dot_general(a,b,dn,preferred_element_type=f32)

def lane_half(x, hh):
    lane=lax.broadcasted_iota(jnp.int32, x.shape, 1)
    keep=(lane<64) if hh==0 else (lane>=64)
    return jnp.where(keep, x, jnp.zeros_like(x))

def gelu_pair(u):
    u2=u*u
    t=jnp.tanh(gc*(u+0.044715*u2*u))
    return 0.5*u*(1.0+t), 0.5*(1.0+t)+0.5*u*(1.0-t*t)*gc*(1.0+3.0*0.044715*u2)
def nrm(v):
    c=v-jnp.mean(v,axis=-1,keepdims=True)
    r=lax.rsqrt(jnp.mean(c*c,axis=-1,keepdims=True)+1e-6)
    return c*r,r
def rows_loop(n, R, f):
    def body(i,_):
        f(pl.ds(pl.multiple_of(i*R,R),R)); return 0
    lax.fori_loop(0,n//R,body,0)

def kb_kernel(R, tok, gout, attnT, mod, bias, bup, wall,
      bo_ref, dx1_ref, dat_ref, dw_h, dwout_ref, dmod_ref, db_ref, dbup_ref,
      h2, h2T, dzb, dzT, z, dh2, o_s, wout, wbuf, act, du, dwst, wsem, osem, wosem):
    def co(g): return pltpu.make_async_copy(wall.at[g, :, 768:1024], wout.at[:, g*256:(g+1)*256], wosem.at[g])
    for g in range(4): co(g).start()
    def fetch(j, slot):
        pltpu.make_async_copy(wall.at[4 + j], wbuf.at[slot], wsem.at[slot]).start()
    fetch(0,0)
    shift1=mod[0:1];scale1=mod[1:2];gate1=mod[2:3];shift2=mod[3:4];scale2=mod[4:5];gate2=mod[5:6]
    db_ref[...]=jnp.zeros_like(db_ref); dmod_ref[...]=jnp.zeros_like(dmod_ref)
    for g in range(4): co(g).wait()
    def pre(r):
        o=dot(attnT[:,r],wout[...],TN)+bias[2:3]
        o_s[r,:]=o
        x1=tok[r,:].astype(f32)+gate1*o
        xh,_=nrm(x1)
        h2[r,:]=(xh*(1.0+scale2)+shift2).astype(bf)
        dz=gout[r,:].astype(f32)*gate2
        dzb[r,:]=dz.astype(bf)
        db_ref[3:4]+=jnp.sum(dz,axis=0,keepdims=True)
    rows_loop(S,256,pre)
    for i in range(4):
        r=slice(i*256,(i+1)*256)
        h2T[:,r]=h2[r,:].T
        dzT[:,r]=dzb[r,:].T
    z[...]=jnp.zeros_like(z); dh2[...]=jnp.zeros_like(dh2)
    def chunk(j,_):
        slot=lax.rem(j,2)
        @pl.when(j+1<NJ)
        def _(): fetch(j+1,1-slot)
        pltpu.make_async_copy(wall.at[4 + j], wbuf.at[slot], wsem.at[slot]).wait()
        dbup_ref[j]=jnp.zeros((1,CH),f32)
        def row(r):
            u=dot(h2[r,:],wbuf[slot,:,:CH])+bup[j]
            a,sl=gelu_pair(u)
            ab=a.astype(bf); act[r,:]=ab
            da=dot(dzb[r,:],wbuf[slot,:,CH:])
            d=da*sl
            dbup_ref[j]+=jnp.sum(d,axis=0,keepdims=True)
            db_=d.astype(bf); du[r,:]=db_
            z[r,:]+=dot(ab,wbuf[slot,:,CH:],NT)
            dh2[r,:]+=dot(db_,wbuf[slot,:,:CH],NT)
        rows_loop(S,R,row)
        @pl.when(j>=2)
        def _():
            pltpu.make_async_copy(dwst.at[slot], dw_h.at[j], osem.at[slot]).wait()
        def wrow(r):
            dwst[slot,0,r,:]=dot(h2T[r,:],du[...])
            dwst[slot,1,r,:]=dot(dzT[r,:],act[...])
        rows_loop(D,256,wrow)
        pltpu.make_async_copy(dwst.at[slot], dw_h.at[j], osem.at[slot]).start()
        return 0
    lax.fori_loop(0,NJ,chunk,0)
    for s in range(2): pltpu.make_async_copy(dwst.at[s], dw_h.at[s], osem.at[s]).wait()
    def post(r):
        g=gout[r,:].astype(f32); o=o_s[r,:]
        x1=tok[r,:].astype(f32)+gate1*o
        xh,rstd=nrm(x1)
        zz=z[r,:]+bias[3:4]
        bo_ref[r,:]=(x1+gate2*zz).astype(bf)
        dmod_ref[5:6]+=jnp.sum(g*zz,axis=0,keepdims=True)
        dh=dh2[r,:]
        dmod_ref[3:4]+=jnp.sum(dh,axis=0,keepdims=True)
        dmod_ref[4:5]+=jnp.sum(dh*xh,axis=0,keepdims=True)
        gg=dh*(1.0+scale2)
        dx1=g+rstd*(gg-jnp.mean(gg,axis=-1,keepdims=True)-xh*jnp.mean(gg*xh,axis=-1,keepdims=True))
        dx1_ref[r,:]=dx1
        dmod_ref[2:3]+=jnp.sum(dx1*o,axis=0,keepdims=True)
        do=dx1*gate1
        db_ref[2:3]+=jnp.sum(do,axis=0,keepdims=True)
        dob=do.astype(bf)
        dzb[r,:]=dob
        t=dot(dob,wout[...],NT).astype(bf)
        for g4 in range(4): dat_ref[g4,r,:]=t[:,g4*256:(g4+1)*256]
    rows_loop(S,128,post)
    def wo(r):
        dwout_ref[r,:]=dot(attnT[r,:],dzb[...])
    rows_loop(D,256,wo)

def kb(R,*a):
    V=pl.BlockSpec(memory_space=pltpu.VMEM); A=pl.BlockSpec(memory_space=pl.ANY)
    sd=jax.ShapeDtypeStruct
    return pl.pallas_call(functools.partial(kb_kernel,R),
      out_shape=(sd((S,D),bf),sd((S,D),f32),sd((4,S,256),bf),sd((NJ,2,D,CH),f32),sd((D,D),f32),sd((8,D),f32),sd((8,D),f32),sd((NJ,1,CH),f32)),
      in_specs=[V]*6+[A], out_specs=[V,V,V,A,V,V,V,V],
      scratch_shapes=[pltpu.VMEM((S,D),bf)]*4+[pltpu.VMEM((S,D),f32)]*3+[pltpu.VMEM((D,D),bf),pltpu.VMEM((2,D,2*CH),bf),pltpu.VMEM((S,CH),bf),pltpu.VMEM((S,CH),bf),
         pltpu.VMEM((2,2,D,CH),f32),pltpu.SemaphoreType.DMA((2,)),pltpu.SemaphoreType.DMA((2,)),pltpu.SemaphoreType.DMA((4,))],
      compiler_params=pltpu.CompilerParams(vmem_limit_bytes=62*2**20), name=f"kb{R}")(*a)

def ka_kernel(tok, mod, bqkv, wall, qkv, attnT, lse, h1T, h1, wbuf, wsem):
    c = LOG2E / 8.0

    def cp(g, slot):
        return pltpu.make_async_copy(wall.at[g, :, 0:768], wbuf.at[slot], wsem.at[slot])

    cp(0, 0).start()
    shift1, scale1 = mod[0:1], mod[1:2]

    def ln(r):
        xh, _ = nrm(tok[r, :].astype(f32))
        h1[r, :] = (xh * (1.0 + scale1) + shift1).astype(bf)

    rows_loop(S, 128, ln)
    for i in range(4):
        r = slice(i * 256, (i + 1) * 256)
        h1T[:, r] = h1[r, :].T

    def group(g, _):
        slot = lax.rem(g, 2)
        when(g < 3, lambda: cp(g + 1, 1 - slot).start())
        cp(g, slot).wait()

        def proj(r):
            qkv[g, r, :] = (dot(h1[r, :], wbuf[slot]) + bqkv[g]).astype(bf)

        rows_loop(S, 256, proj)
        for p in range(2):
            kp = qkv[g, :, 256 + p * 128 : 256 + (p + 1) * 128]
            vT = qkv[g, :, 512 + p * 128 : 512 + (p + 1) * 128].T
            q = qkv[g, :, p * 128 : (p + 1) * 128]
            for h in range(2):
                s = dot(lane_half(kp, h), q, NT)
                m = jnp.max(s, axis=0, keepdims=True)
                e = jnp.exp2((s - m) * c)
                l = jnp.sum(e, axis=0, keepdims=True)
                pr = (e * (1.0 / l)).astype(bf)
                o = dot(vT[h * 64 : (h + 1) * 64], pr)
                lse[g, p * 2 + h : p * 2 + h + 1, :] = m * 0.125 + jnp.log(l)
                attnT[pl.ds(pl.multiple_of(g * 256 + (p * 128 + h * 64), 64), 64), :] = o.astype(bf)
        return 0

    lax.fori_loop(0, 4, group, 0)


def ka(*a):
    return pl.pallas_call(
        ka_kernel,
        out_shape=(sd((4, S, 768), bf), sd((D, S), bf), sd((4, 4, S), f32), sd((D, S), bf)),
        in_specs=[V, V, V, A],
        out_specs=[V] * 4,
        scratch_shapes=[pltpu.VMEM((S, D), bf), pltpu.VMEM((2, D, 768), bf), pltpu.SemaphoreType.DMA((2,))],
        compiler_params=pltpu.CompilerParams(vmem_limit_bytes=60 * 2**20),
        name="attention_forward",
    )(*a)


def kc_kernel(QB, tok, mod, qkv, dat, lse, dx1, h1T, w_h, ig, dw_h, dmod, dbq, dqkv, dk_s, dv_s, dqT_s, dh1, wbuf, dwst, wsem, osem):
    c=LOG2E/8.0
    def cp(g,slot): return pltpu.make_async_copy(w_h.at[g, :, 0:768], wbuf.at[slot], wsem.at[slot])
    def co(g,slot): return pltpu.make_async_copy(dwst.at[slot], dw_h.at[g], osem.at[slot])
    cp(0,0).start()
    dh1[...]=jnp.zeros_like(dh1); dmod[...]=jnp.zeros_like(dmod); dbq[...]=jnp.zeros_like(dbq)
    def group(g,_):
        slot=lax.rem(g,2)
        @pl.when(g<3)
        def _(): cp(g+1,1-slot).start()
        for p in range(2):
            sl=slice(p*128,(p+1)*128); slk=slice(256+p*128,256+(p+1)*128); slv=slice(512+p*128,512+(p+1)*128)
            kp=qkv[g,:,slk]; vp=qkv[g,:,slv]
            ks=[lane_half(kp,h) for h in range(2)]; vs=[lane_half(vp,h) for h in range(2)]
            kT=kp.T
            dk_s[...]=jnp.zeros_like(dk_s); dv_s[...]=jnp.zeros_like(dv_s)
            def qblk(i,_):
                r=pl.ds(pl.multiple_of(i*QB,QB),QB)
                q=qkv[g,r,sl]; da=dat[g,r,sl]
                for h in range(2):
                    s=dot(ks[h],q,NT)
                    pT=jnp.exp2(s*c-lse[g,p*2+h:p*2+h+1,r]*LOG2E)
                    dp=dot(vs[h],da,NT)
                    delta=jnp.sum(pT*dp,axis=0,keepdims=True)
                    ds=(pT*(dp-delta)).astype(bf)
                    dv_s[...]+=dot(pT.astype(bf),lane_half(da,h))
                    dk_s[...]+=dot(ds,lane_half(q,h))
                    dqT_s[h*64:(h+1)*64,r]=dot(kT[h*64:(h+1)*64],ds)
                return 0
            lax.fori_loop(0,S//QB,qblk,0)
            dq=dqT_s[...].T*0.125
            dbq[g,:,sl]=jnp.sum(dq,axis=0,keepdims=True)
            dqkv[:,sl]=dq.astype(bf)
            dqkv[:,slk]=(dk_s[...]*0.125).astype(bf)
            dbq[g,:,slv]=jnp.sum(dv_s[...],axis=0,keepdims=True)
            dqkv[:,slv]=dv_s[...].astype(bf)
        cp(g,slot).wait()
        @pl.when(g>=2)
        def _(): co(g,slot).wait()
        def wrow(r):
            dwst[slot,r,:]=dot(h1T[r,:],dqkv[...])
            dh1[r,:]+=dot(dqkv[r,:],wbuf[slot],NT)
        rows_loop(D,256,wrow)
        co(g,slot).start()
        return 0
    lax.fori_loop(0,4,group,0)
    for s_ in range(2): co(s_,s_).wait()
    scale1=mod[1:2]
    def post(r):
        xh,rstd=nrm(tok[r,:].astype(f32))
        dh=dh1[r,:]
        dmod[0:1]+=jnp.sum(dh,axis=0,keepdims=True)
        dmod[1:2]+=jnp.sum(dh*xh,axis=0,keepdims=True)
        gg=dh*(1.0+scale1)
        ig[r,:]=dx1[r,:]+rstd*(gg-jnp.mean(gg,axis=-1,keepdims=True)-xh*jnp.mean(gg*xh,axis=-1,keepdims=True))
    rows_loop(S,128,post)
def kc(QB,*a):
    return pl.pallas_call(functools.partial(kc_kernel,QB),
      out_shape=(sd((S,D),f32),sd((4,D,768),f32),sd((8,D),f32),sd((4,1,768),f32)),
      in_specs=[V]*7+[A], out_specs=[V,A,V,V],
      scratch_shapes=[pltpu.VMEM((S,768),bf),pltpu.VMEM((S,128),f32),pltpu.VMEM((S,128),f32),pltpu.VMEM((128,S),f32),pltpu.VMEM((S,D),f32),
        pltpu.VMEM((2,D,768),bf),pltpu.VMEM((2,D,768),f32),pltpu.SemaphoreType.DMA((2,)),pltpu.SemaphoreType.DMA((2,))],
      compiler_params=pltpu.CompilerParams(vmem_limit_bytes=60*2**20), name=f"kc{QB}")(*a)
def when(cond, f):
    @pl.when(cond)
    def _():
        f()


class Pair:
    def __init__(self, at, own, theirs, send, recv, credit, count):
        self.at, self.own, self.theirs, self.sems, self.credit, self.count = at, own, theirs, (send, recv), credit, count

    def copy(self, i, part, cols):
        slot = lax.rem(i, 2)
        return remote(self.own.at[slot, :, cols], self.theirs.at[slot, :, cols], self.sems[0].at[slot, part], self.sems[1].at[slot, part], self.at.to_c)

    def start(self, i, part, cols):
        if part == 0:
            when(i >= 2, lambda: pl.semaphore_wait(self.credit, 1))
        self.copy(i, part, cols).start()

    def sent(self, i, parts):
        for part, cols in enumerate(parts):
            self.copy(i, part, cols).wait_send()

    def arrived(self, i, parts):
        for part, cols in enumerate(parts):
            self.copy(i, part, cols).wait_recv()

    def free(self, i):
        when(i + 2 < self.count, lambda: mesh_signal(self.credit, self.at.to_c))


WHOLE = (slice(0, 1024),)
PARTS = (slice(768, 1024), slice(0, 384), slice(384, 768))


class Scatter:
    shapes = [
        pltpu.VMEM((2, 2, 2, 2, 32, 1024), f32),
        pltpu.VMEM((2, 2, 2, 2, 16, 1024), bf),
        pltpu.VMEM((2, 2, 2, 2, 16, 1024), f32),
        pltpu.VMEM((2, 2, 2, 2, 2, 16, 1024), bf),
        pltpu.VMEM((2, 2, 2, 16, 1024), bf),
        pltpu.VMEM((2, 2, 2, 16, 1024), f32),
        pltpu.VMEM((2, 2, 2, 2, 16, 1024), bf),
        pltpu.VMEM((2, 32, 1024), f32),
        pltpu.VMEM((2, 32, 1024), f32),
        pltpu.VMEM((2, 2, 32, 1024), f32),
        pltpu.VMEM((32, 1024), f32),
        pltpu.VMEM((32, 1024), f32),
        pltpu.VMEM((2, 32, 1024), f32),
        pltpu.SemaphoreType.DMA((6,)),
        pltpu.SemaphoreType.DMA((2, 6)),
        pltpu.SemaphoreType.REGULAR((6,)),
    ]

    def __init__(self, at, refs, out, count, gaps=()):
        self.at, self.out, self.count, self.gaps = at, out, count, gaps
        self.acc, self.s2, self.k2, self.r2, self.s3, self.k3, self.r3, self.s4, self.k4, self.r4, self.s5, self.k5, self.r5, self.send, self.recv, self.credit = refs

    def todo(self, stage, slot):
        at = self.at
        if stage == 2:
            return [(0, self.s2.at[0], self.r2.at[slot, 0], at.to_y), (1, self.s2.at[1], self.r2.at[slot, 1], at.to_x)]
        if stage == 3:
            return [(2, self.s3.at[0], self.r3.at[slot, 0], at.to_x), (3, self.s3.at[1], self.r3.at[slot, 1], at.to_y)]
        if stage == 4:
            return [(4, self.s4, self.r4.at[slot], at.to_b)]
        return [(5, self.s5, self.r5.at[slot], at.to_a)]

    def copies(self, stage, i):
        slot = lax.rem(i, 2)
        return [remote(src, dst, self.send.at[q], self.recv.at[slot, q], dev) for q, src, dst, dev in self.todo(stage, slot)]

    def reuse(self, stage, i):
        def go():
            for cp in self.copies(stage, i - 1):
                cp.wait_send()

        when(i >= 1, go)

    def start(self, stage, i):
        def go():
            for q, _, _, _ in self.todo(stage, 0):
                pl.semaphore_wait(self.credit.at[q], 1)

        when(i >= 2, go)
        for cp in self.copies(stage, i):
            cp.start()

    def arrived(self, stage, i):
        for cp in self.copies(stage, i):
            cp.wait_recv()

    def free(self, stage, i):
        def go():
            for q, _, _, dev in self.todo(stage, 0):
                mesh_signal(self.credit.at[q], dev)

        when(i + 2 < self.count, go)

    def two(self, i, acc):
        y, x = self.at.y, self.at.x
        lo, hi = pl.ds(0, 16), pl.ds(16, 16)
        self.reuse(2, i)
        self.s2[0] = acc[:, :, 1 - y, :, lo, :].astype(bf)
        self.s2[1] = acc[:, :, :, 1 - x, hi, :].astype(bf)
        self.start(2, i)
        self.k2[0] = acc[:, :, y, :, lo, :]
        self.k2[1] = acc[:, :, :, x, hi, :]

    def three(self, i):
        y, x = self.at.y, self.at.x
        slot = lax.rem(i, 2)
        self.arrived(2, i)
        self.reuse(3, i)
        self.s3[0] = (self.k2[0, :, :, 1 - x] + self.r2[slot, 0, :, :, 1 - x].astype(f32)).astype(bf)
        self.s3[1] = (self.k2[1, :, :, 1 - y] + self.r2[slot, 1, :, :, 1 - y].astype(f32)).astype(bf)
        self.start(3, i)
        self.k3[0] = self.k2[0, :, :, x] + self.r2[slot, 0, :, :, x].astype(f32)
        self.k3[1] = self.k2[1, :, :, y] + self.r2[slot, 1, :, :, y].astype(f32)
        self.free(2, i)

    def four(self, i):
        b = self.at.b
        slot = lax.rem(i, 2)
        self.arrived(3, i)
        self.reuse(4, i)
        for h in (0, 1):
            rows = slice(16 * h, 16 * h + 16)
            self.s4[:, rows, :] = self.k3[h, :, 1 - b] + self.r3[slot, h, :, 1 - b].astype(f32)
        self.start(4, i)
        for h in (0, 1):
            rows = slice(16 * h, 16 * h + 16)
            self.k4[:, rows, :] = self.k3[h, :, b] + self.r3[slot, h, :, b].astype(f32)
        self.free(3, i)

    def five(self, i):
        a = self.at.a
        slot = lax.rem(i, 2)
        self.arrived(4, i)
        self.reuse(5, i)
        self.s5[...] = self.k4[1 - a] + self.r4[slot, 1 - a]
        self.start(5, i)
        self.k5[...] = self.k4[a] + self.r4[slot, a]
        self.free(4, i)

    def six(self, i):
        slot = lax.rem(i, 2)
        self.arrived(5, i)
        t = self.k5[...] + self.r5[slot]

        def spread(start, src, width):
            self.out[:, pl.ds(pl.multiple_of(start, 128), width)] = t[:, src : src + width]

        def feed_forward():
            spread(4 * D + i * CH, 0, CH)
            spread(4 * D + FF + i * CH, CH, CH)

        def attention():
            g = i - NJ
            for p in range(2):
                for q in range(3):
                    spread(q * D + g * 256 + p * 128, p * 384 + q * 128, 128)
            spread(3 * D + g * 256, 768, 256)

        when(i < NJ, feed_forward)
        when(i >= NJ, attention)
        self.free(5, i)

    def tick(self, t):
        for lag, f in ((4, self.six), (3, self.five), (2, self.four), (1, self.three)):
            u = t - lag
            live = (u >= 0) & (u < self.count + len(self.gaps))
            piece = u
            for gap in self.gaps:
                live = live & (u != gap)
                piece = piece - jnp.where(u > gap, 1, 0)
            when(live, functools.partial(f, piece))

    def finish(self):
        for stage in (2, 3, 4, 5):
            for cp in self.copies(stage, self.count - 1):
                cp.wait_send()


def block_kernel(n, tok, gout, small, weights,
                 bo, ig, gw, bsum, dsum, crec, wall, dwh, qkvh, dath,
                 mine, ada, gat, condc, rec, dsrc, dall, lsrc, lall, esrc, erec, csrc, mod, brow, bqkv, bup, dmod, db, dbup, dbq,
                 attnT, h1T, lse, dob, dx1, own, theirs, halfS,
                 s0, r0, s2, r2, s3, r3, s4, r4, s5, r5, s6, r6, xs, xr, ps, pr, pc, hc, wsem, qsem, osem, stsem, local, send, recv, *sc):
    c = LOG2E / 8.0
    at = Place()
    me = at.me
    gather = Gather(at, mine, wall, local, send, recv, 12)
    pair = Pair(at, own, theirs, ps, pr, pc, NJ + 4)
    scatter = Scatter(at, sc, gw, 12, gaps=(11,))

    def cut(shard):
        load = pltpu.make_async_copy(weights, shard, osem.at[0])
        load.start()
        load.wait()
        for g in range(4):
            for p in range(2):
                for q in range(3):
                    a = q * D + g * 256 + p * 128
                    b = p * 384 + q * 128
                    mine[g, :, b : b + 128] = shard[:, a : a + 128].astype(bf)
            mine[g, :, 768:] = shard[:, 3 * D + g * 256 : 3 * D + (g + 1) * 256].astype(bf)
        gather.start(0, 4)
        for j in range(NJ):
            for q in range(2):
                a = 4 * D + q * FF + j * CH
                mine[4 + j, :, q * CH : (q + 1) * CH] = shard[:, a : a + CH].astype(bf)
        gather.start(4, 12)
        for q in range(6):
            a = 4 * D + 2 * FF + q * D
            ada[at.c, :, q * D : (q + 1) * D] = shard[:, a : a + D].astype(bf)

    greet_all(n, me, lambda: pl.run_scoped(cut, pltpu.VMEM((32, 18 * D), f32)))
    gather.tick(0)
    trade_ada = remote(ada.at[at.c], ada.at[at.c], xs.at[4], xr.at[4], at.to_c)
    trade_ada.start()
    each_peer(n, me, lambda k, to, fr: remote(small, gat.at[me // 2, at.c], s0.at[k], r0.at[k], to).start())
    gat[pl.ds(me // 2, 1), pl.ds(at.c, 1)] = small[...].reshape(1, 1, 16, 128)
    db[...] = jnp.zeros_like(db)
    dmod[...] = jnp.zeros_like(dmod)

    def bias_into(biases, ref, row, start, lead):
        for q in range(lead):
            k = start + q
            ref[row, :, q * 64 : (q + 1) * 64] = biases[k // 7, k % 7 : k % 7 + 1, 0:64]

    def fetch(i, wbuf, slot):
        return pltpu.make_async_copy(wall.at[i], wbuf.at[slot], wsem.at[slot])

    def bias_from(k, piece):
        esrc[k // 7, :, (k % 7) * 64 : (k % 7 + 1) * 64] = piece

    def ada_columns(x, q):
        cols = slice(q * 512, (q + 1) * 512)
        gw[:, 4 * D + 2 * FF + q * 512 : 4 * D + 2 * FF + (q + 1) * 512] = dot(condc[...], x, TN)
        return dot(x, ada[pl.ds(at.c, 1), :, cols].reshape(32, 512), NT)

    def qkv_out(g, qkv):
        return pltpu.make_async_copy(qkv.at[lax.rem(g, 2)], qkvh.at[g], qsem.at[lax.rem(g, 2)])

    def qkv_in(g, qkv):
        return pltpu.make_async_copy(qkvh.at[g], qkv.at[lax.rem(g, 2)], qsem.at[lax.rem(g, 2)])

    def matrix(wbuf, slot, cols):
        return wbuf[slot, :, :, :, :, :, cols].reshape(D, cols.stop - cols.start)

    lead, tail = pl.ds(0, 2 * D), pl.ds(2 * D, 4 * D)

    def attention(h1, wbuf, qkv, part, biases, conds):
        def norm_one(r):
            xh, _ = nrm(tok[r, :].astype(f32))
            dx1[r, :] = xh

        rows_loop(S, 256, norm_one)
        each_peer(n, me, lambda k, to, fr: remote(small, gat.at[fr // 2, lax.rem(fr, 2)], s0.at[k], r0.at[k], to).wait())
        biases[...] = gat[...].astype(f32).reshape(n, 16, 128)[:, 8:16]
        conds[...] = gat[...].astype(f32).reshape(n // 2, 2, 16, 128)[:, :, 0:8]
        lane = lax.broadcasted_iota(jnp.int32, (128, 64), 0)
        want = lax.rem(me // 2, 2) * 64 + lax.broadcasted_iota(jnp.int32, (128, 64), 1)
        pick = jnp.where(lane == want, 1.0, 0.0).astype(bf)
        wanted = conds[:, :, pl.ds(me // 4, 1), :].reshape(n, 128).astype(bf)
        both = dot(wanted, pick)
        condc[...] = jnp.where(at.c == 0, both[:, 0:32], both[:, 32:64]).astype(bf)
        mates = dot(conds[:, pl.ds(at.c, 1), pl.ds(me // 4, 1), :].reshape(n // 2, 128).astype(bf), pick).astype(bf)
        trade_ada.wait_send()
        remote(ada.at[at.c], ada.at[1 - at.c], xs.at[4], xr.at[4], at.to_c).wait_recv()

        def columns(q):
            cols = slice(q * 512, (q + 1) * 512)
            part[:, :, cols] = dot(mates, ada[:, :, cols].reshape(64, 512)).reshape(n // 2, 1, 512)

        for q in range(4):
            columns(q)
        each_mate(n, me, lambda k, to, fr: remote(part.at[to // 2, :, lead], rec.at[me // 2, :, lead], s2.at[0, k], r2.at[0, k], to).start())
        gather.tick(1)
        for q in range(4, 12):
            columns(q)
        rec[pl.ds(me // 2, 1)] = part[pl.ds(me // 2, 1)]
        for q in range(6):
            bias_into(biases, mod, q, 128 + 16 * q, 16)
        bias_into(biases, brow, 0, 32, 16)
        bias_into(biases, brow, 1, 112, 16)
        for j in range(NJ):
            bias_into(biases, bup, j, 48 + 8 * j, 8)
        for g in range(4):
            bqkv[g] = jnp.zeros((1, 768), f32)
            for q in range(4):
                for first, offset in ((0, 0), (16, 256)):
                    k = first + g * 4 + q
                    to = (q // 2) * 384 + offset + (q % 2) * 64
                    bqkv[g, :, to : to + 64] = biases[k // 7, k % 7 : k % 7 + 1, 0:64]
        gather.tick(2)
        each_mate(n, me, lambda k, to, fr: remote(part.at[to // 2, :, lead], rec.at[fr // 2, :, lead], s2.at[0, k], r2.at[0, k], to).wait())
        each_mate(n, me, lambda k, to, fr: remote(part.at[to // 2, :, tail], rec.at[me // 2, :, tail], s2.at[1, k], r2.at[1, k], to).start())
        for q in range(2):
            mod[q] += jnp.sum(rec[:, :, q * D : (q + 1) * D], axis=0)
        shift1, scale1 = mod[0], mod[1]

        def modulate(r):
            h1[r, :] = (dx1[r, :] * (1.0 + scale1) + shift1).astype(bf)

        rows_loop(S, 256, modulate)
        for i in range(4):
            r = slice(i * 256, (i + 1) * 256)
            h1T[:, :, :, r] = h1[r, :].T.reshape(16, 2, 32, 256)
        gather.tick(3, (4,))
        gather.tick(4, (5,))
        fetch(0, wbuf, 0).start()
        gather.tick(3, (3, 2, 1))

        def group(g, _):
            slot = lax.rem(g, 2)
            fetch(g, wbuf, slot).wait()
            when(g >= 2, lambda: qkv_out(g - 2, qkv).wait())
            w = matrix(wbuf, slot, slice(0, 768))

            def proj(r):
                qkv[slot, r, :] = (dot(h1[r, :], w) + bqkv[g]).astype(bf)

            for r in (slice(0, 512), slice(512, 1024)):
                proj(r)
            qkv_out(g, qkv).start()
            when(g == 0, lambda: gather.tick(4, (4, 3, 2, 1)))
            for p in range(2):
                kp = qkv[slot, :, p * 384 + 128 : p * 384 + 256]
                vT = qkv[slot, :, p * 384 + 256 : p * 384 + 384].T
                q = qkv[slot, :, p * 384 : p * 384 + 128]
                scores = [dot(lane_half(kp, h), q, NT) for h in range(2)]
                probs = []
                for h in range(2):
                    m = jnp.max(scores[h], axis=0, keepdims=True)
                    e = jnp.exp2((scores[h] - m) * c)
                    l = jnp.sum(e, axis=0, keepdims=True)
                    probs.append((e * (1.0 / l)).astype(bf))
                    lse[g, p * 2 + h : p * 2 + h + 1, :] = m * 0.125 + jnp.log(l)
                for h in range(2):
                    o = dot(vT[h * 64 : (h + 1) * 64], probs[h])
                    attnT[pl.ds(g * 4 + p * 2 + h, 1)] = o.astype(bf).reshape(1, 2, 32, S)
            gather.tick(5 + g)
            when(g < 3, lambda: fetch(g + 1, wbuf, 1 - slot).start())
            return 0

        lax.fori_loop(0, 4, group, 0)
        for g in (2, 3):
            qkv_out(g, qkv).wait()
        each_mate(n, me, lambda k, to, fr: remote(part.at[to // 2, :, tail], rec.at[fr // 2, :, tail], s2.at[1, k], r2.at[1, k], to).wait())
        for q in range(2, 6):
            mod[q] += jnp.sum(rec[:, :, q * D : (q + 1) * D], axis=0)

    pl.run_scoped(
        attention,
        pltpu.VMEM((S, D), bf),
        pltpu.VMEM((2, 4, 2, 2, 2, 32, 1024), bf),
        pltpu.VMEM((2, S, 768), bf),
        pltpu.VMEM((n // 2, 1, 6 * D), f32),
        pltpu.VMEM((n, 8, 128), f32),
        pltpu.VMEM((n // 2, 2, 8, 128), f32),
    )

    def unstage(i):
        return pltpu.make_async_copy(dwh.at[i], scatter.acc, stsem.at[1])

    def staged(i):
        unstage(i).wait()
        scatter.two(i, scatter.acc)
        when(i + 1 < NJ, lambda: unstage(i + 1).start())

    def mlp(h2, hT, dzT, z, wout, wbuf, accw):
        gate1, shift2, scale2, gate2 = mod[2], mod[3], mod[4], mod[5]

        def stage(i):
            return pltpu.make_async_copy(accw, dwh.at[i], stsem.at[0])

        def co(g):
            return pltpu.make_async_copy(wall.at[g, :, :, :, :, :, 768:1024], wout.at[:, :, :, :, :, g * 256 : (g + 1) * 256], osem.at[g])

        for g in range(4):
            co(g).start()
        fetch(4, wbuf, 0).start()
        for g in range(4):
            co(g).wait()

        def branch(r):
            width = r.size
            return dot(attnT[:, :, :, r].reshape(D, width), wout[...].reshape(D, D), TN) + brow[0]

        def pre(r):
            x1 = tok[r, :].astype(f32) + gate1 * branch(r)
            xh, _ = nrm(x1)
            h2[r, :] = (xh * (1.0 + scale2) + shift2).astype(bf)
            dz = gout[r, :].astype(f32) * gate2
            dob[r, :] = dz.astype(bf)
            db[1] += jnp.sum(dz, axis=0, keepdims=True)

        def pre_block(i, _):
            pre(pl.ds(pl.multiple_of(i * 256, 256), 256))
            when(i == 1, lambda: gather.tick(9, (5, 3)))
            when(i == 3, lambda: gather.tick(9, (4, 2, 1)))
            return 0

        lax.fori_loop(0, 4, pre_block, 0)
        for i in range(4):
            r = slice(i * 256, (i + 1) * 256)
            hT[:, :, :, r] = h2[r, :].T.reshape(16, 2, 32, 256)
            dzT[:, :, :, r] = dob[r, :].T.reshape(16, 2, 32, 256)
        halves = [
            remote(hT.at[:, 1 - at.c], halfS.at[0], xs.at[0], xr.at[0], at.to_c),
            remote(dzT.at[:, 1 - at.c], halfS.at[1], xs.at[1], xr.at[1], at.to_c),
        ]
        for cp in halves:
            cp.start()
        z[...] = jnp.zeros_like(z)
        dx1[...] = jnp.zeros_like(dx1)

        def chunk(j, _):
            when(j >= 1, lambda: gather.tick(9 + j, (4, 2, 1)))

            def forward():
                slot = lax.rem(j, 2)
                when(j + 1 < NJ, lambda: fetch(5 + j, wbuf, 1 - slot).start())
                fetch(4 + j, wbuf, slot).wait()
                when(j >= 2, lambda: pair.sent(j - 2, WHOLE))
                dbup[j] = jnp.zeros((1, CH), f32)

                w_up, w_dn = matrix(wbuf, slot, slice(0, CH)), matrix(wbuf, slot, slice(CH, 2 * CH))
                blocks = (slice(0, 512), slice(512, 1024))
                ups = [dot(h2[r, :], w_up) + bup[j] for r in blocks]
                backs = [dot(dob[r, :], w_dn) for r in blocks]
                for r, u, back_ in zip(blocks, ups, backs):
                    a, sl = gelu_pair(u)
                    ab = a.astype(bf)
                    own[slot, r, CH:] = ab
                    d = back_ * sl
                    dbup[j] += jnp.sum(d, axis=0, keepdims=True)
                    db_ = d.astype(bf)
                    own[slot, r, :CH] = db_
                    z[r, :] += dot(ab, w_dn, NT)
                    dx1[r, :] += dot(db_, w_up, NT)

                pair.start(j, 0, WHOLE[0])

            when(j < NJ, forward)
            gather.tick(10 + j, (5, 3))
            scatter.tick(j - 5)
            when(j >= 5, lambda: staged(j - 5))
            when(j == 4, lambda: unstage(0).start())

            def weights():
                i = j - 1
                slot = lax.rem(i, 2)
                when(j == 1, lambda: [cp.wait_recv() for cp in halves])
                pair.arrived(i, WHOLE)
                when(i >= 1, lambda: stage(i - 1).wait())
                for q, lhs in enumerate((hT, dzT)):
                    cols = slice(q * CH, (q + 1) * CH)
                    t = dot(lhs[:, at.c].reshape(512, S), own[slot, :, cols]) + dot(halfS[q].reshape(512, S), theirs[slot, :, cols])
                    accw[:, :, :, :, :, cols] = t.reshape(2, 2, 2, 2, 32, CH)
                pair.free(i)
                stage(i).start()

            when(j >= 1, weights)
            return 0

        lax.fori_loop(0, NJ + 1, chunk, 0)
        mesh_signal(hc, at.to_c)
        stage(NJ - 1).wait()
        for cp in halves:
            cp.wait_send()

        def post(r):
            g = gout[r, :].astype(f32)
            o = branch(r)
            x1 = tok[r, :].astype(f32) + gate1 * o
            xh, rstd = nrm(x1)
            zz = z[r, :] + brow[1]
            h2[r, :] = (x1 + gate2 * zz).astype(bf)
            dmod[5] += jnp.sum(g * zz, axis=0, keepdims=True)
            dh = dx1[r, :]
            dmod[3] += jnp.sum(dh, axis=0, keepdims=True)
            dmod[4] += jnp.sum(dh * xh, axis=0, keepdims=True)
            gg = dh * (1.0 + scale2)
            dx = g + rstd * (gg - jnp.mean(gg, axis=-1, keepdims=True) - xh * jnp.mean(gg * xh, axis=-1, keepdims=True))
            dx1[r, :] = dx
            dmod[2] += jnp.sum(dx * o, axis=0, keepdims=True)
            do = dx * gate1
            db[0] += jnp.sum(do, axis=0, keepdims=True)
            dob_ = do.astype(bf)
            dob[r, :] = dob_
            own[0, r, :] = dot(dob_, wout[...].reshape(D, D), NT).astype(bf)

        pair.sent(NJ - 2, WHOLE)

        def post_half(h):
            def body(i, _):
                post(pl.ds(pl.multiple_of(h * 512 + i * 256, 256), 256))
                return 0

            lax.fori_loop(0, 2, body, 0)

        post_half(0)
        post_half(1)
        outs = [pltpu.make_async_copy(h2, bo, osem.at[0])]
        outs += [pltpu.make_async_copy(own.at[0, :, g * 256 : (g + 1) * 256], dath.at[g], osem.at[1 + g]) for g in range(4)]
        for cp in outs:
            cp.start()
        for cp in outs:
            cp.wait()

    pl.run_scoped(
        mlp,
        pltpu.VMEM((S, D), bf),
        pltpu.VMEM((16, 2, 32, S), bf),
        pltpu.VMEM((16, 2, 32, S), bf),
        pltpu.VMEM((S, D), f32),
        pltpu.VMEM((4, 2, 2, 2, 32, 1024), bf),
        pltpu.VMEM((2, 4, 2, 2, 2, 32, 1024), bf),
        pltpu.VMEM((2, 2, 2, 2, 32, 1024), f32),
    )

    def back(dh1, wbuf, qkv, dat, dk_s, dv_s, dqT_s, accw):
        def dat_in(g):
            return pltpu.make_async_copy(dath.at[g], dat.at[lax.rem(g, 2)], osem.at[lax.rem(g, 2)])

        def load(g):
            qkv_in(g, qkv).start()
            dat_in(g).start()
            fetch(g, wbuf, lax.rem(g, 2)).start()

        load(0)
        pl.semaphore_wait(hc, 1)
        halves = [
            remote(h1T.at[:, 1 - at.c], halfS.at[0], xs.at[2], xr.at[2], at.to_c),
            remote(attnT.at[:, 1 - at.c], halfS.at[1], xs.at[3], xr.at[3], at.to_c),
        ]
        for cp in halves:
            cp.start()
        scatter.tick(4)
        staged(4)
        for q in range(4):
            dsrc[:, q * D : (q + 1) * D] = dmod[2 + q]
        each_mate(n, me, lambda k, to, fr: remote(dsrc, dall.at[at.c, me // 2], s3.at[k], r3.at[k], to).start())
        dall[pl.ds(at.c, 1), pl.ds(me // 2, 1)] = dsrc[...].reshape(1, 1, 1, 4 * D)
        esrc[...] = jnp.zeros_like(esrc)
        for q in range(16):
            bias_from(32 + q, db[0, :, q * 64 : (q + 1) * 64])
            bias_from(112 + q, db[1, :, q * 64 : (q + 1) * 64])
        for j in range(NJ):
            for q in range(8):
                bias_from(48 + 8 * j + q, dbup[j, :, q * 64 : (q + 1) * 64])
        dh1[...] = jnp.zeros_like(dh1)

        def group(g, _):
            slot = lax.rem(g, 2)
            when(g < 3, lambda: load(g + 1))
            qkv_in(g, qkv).wait()
            dat_in(g).wait()
            when(g == 1, lambda: pair.sent(NJ - 1, WHOLE))
            when(g >= 2, lambda: pair.sent(NJ + g - 2, PARTS))
            own[slot, :, 768:] = dob[:, pl.ds(pl.multiple_of(g * 256, 256), 256)]
            pair.start(NJ + g, 0, PARTS[0])
            for p in range(2):
                if p == 1:
                    scatter.tick(5 + 2 * g)
                    when(g < 2, lambda: staged(5 + 2 * g))
                    when(g == 2, lambda: scatter.two(9, accw))
                sl = slice(p * 128, (p + 1) * 128)
                slq, slk, slv = (slice(p * 384 + q * 128, p * 384 + (q + 1) * 128) for q in range(3))
                kp, vp, q, da = qkv[slot, :, slk], qkv[slot, :, slv], qkv[slot, :, slq], dat[slot, :, sl]
                kT = kp.T
                for h in range(2):
                    s = dot(lane_half(kp, h), q, NT)
                    pT = jnp.exp2(s * c - lse[g, p * 2 + h : p * 2 + h + 1, :] * LOG2E)
                    dp = dot(lane_half(vp, h), da, NT)
                    weighted = pT * dp
                    ds = (weighted - pT * jnp.sum(weighted, axis=0, keepdims=True)).astype(bf)
                    dv = dot(pT.astype(bf), lane_half(da, h))
                    dk = dot(ds, lane_half(q, h))
                    if h == 0:
                        dv_s[...] = dv
                        dk_s[...] = dk
                    else:
                        dv_s[...] += dv
                        dk_s[...] += dk
                    dqT_s[h * 64 : (h + 1) * 64, :] = dot(kT[h * 64 : (h + 1) * 64], ds)
                dq = dqT_s[...].T * 0.125
                dbq[g, :, sl] = jnp.sum(dq, axis=0, keepdims=True)
                own[slot, :, slq] = dq.astype(bf)
                own[slot, :, slk] = (dk_s[...] * 0.125).astype(bf)
                dbq[g, :, 256 + p * 128 : 256 + (p + 1) * 128] = jnp.sum(dv_s[...], axis=0, keepdims=True)
                own[slot, :, slv] = dv_s[...].astype(bf)
                pair.start(NJ + g, 1 + p, PARTS[1 + p])
            fetch(g, wbuf, slot).wait()
            w = matrix(wbuf, slot, slice(0, 768))

            def wrow(r):
                dh1[r, :] += dot(own[slot, r, :768], w, NT)

            for r in (slice(0, 512), slice(512, 1024)):
                wrow(r)
            scatter.tick(6 + 2 * g)

            def at_first():
                staged(6)
                for cp in halves:
                    cp.wait_recv()

            when(g == 0, at_first)
            when(g == 1, lambda: scatter.two(8, accw))

            def pass_on():
                each_mate(n, me, lambda k, to, fr: remote(dsrc, dall.at[at.c, fr // 2], s3.at[k], r3.at[k], to).wait())
                remote(dall.at[at.c], dall.at[at.c], xs.at[5], xr.at[5], at.to_c).start()

            when(g == 1, pass_on)
            pair.arrived(NJ + g, PARTS)
            for q, lhs in enumerate((h1T, attnT)):
                cols = slice(0, 768) if q == 0 else slice(768, 1024)
                t = dot(lhs[:, at.c].reshape(512, S), own[slot, :, cols]) + dot(halfS[q].reshape(512, S), theirs[slot, :, cols])
                accw[:, :, :, :, :, cols] = t.reshape(2, 2, 2, 2, 32, cols.stop - cols.start)
            pair.free(NJ + g)
            when(g >= 2, lambda: scatter.two(8 + g, accw))
            return 0

        lax.fori_loop(0, 4, group, 0)
        for g in range(4):
            for q in range(4):
                bias_from(g * 4 + q, dbq[g, :, q * 64 : (q + 1) * 64])
                bias_from(16 + g * 4 + q, dbq[g, :, 256 + q * 64 : 256 + (q + 1) * 64])
        each_peer(n, me, lambda k, to, fr: remote(esrc.at[to], erec.at[me], s4.at[k], r4.at[k], to).start())
        erec[pl.ds(me, 1)] = esrc[pl.ds(me, 1)]
        for i in (2, 3):
            pair.sent(NJ + i, PARTS)
        for cp in halves:
            cp.wait_send()
        scale1 = mod[1]

        def post(r):
            xh, rstd = nrm(tok[r, :].astype(f32))
            dh = dh1[r, :]
            dmod[0] += jnp.sum(dh, axis=0, keepdims=True)
            dmod[1] += jnp.sum(dh * xh, axis=0, keepdims=True)
            gg = dh * (1.0 + scale1)
            dx1[r, :] += rstd * (gg - jnp.mean(gg, axis=-1, keepdims=True) - xh * jnp.mean(gg * xh, axis=-1, keepdims=True))

        rows_loop(S, 256, post)

    pl.run_scoped(
        back,
        pltpu.VMEM((S, D), f32),
        pltpu.VMEM((2, 4, 2, 2, 2, 32, 1024), bf),
        pltpu.VMEM((2, S, 768), bf),
        pltpu.VMEM((2, S, 256), bf),
        pltpu.VMEM((S, 128), f32),
        pltpu.VMEM((S, 128), f32),
        pltpu.VMEM((128, S), f32),
        pltpu.VMEM((2, 2, 2, 2, 32, 1024), f32),
    )
    done = pltpu.make_async_copy(dx1, ig, osem.at[0])
    done.start()
    for k in range(2):
        lsrc[:, k * D : (k + 1) * D] = dmod[k]
    each_mate(n, me, lambda k, to, fr: remote(lsrc, lall.at[at.c, me // 2], s6.at[k], r6.at[k], to).start())
    lall[pl.ds(at.c, 1), pl.ds(me // 2, 1)] = lsrc[...].reshape(1, 1, 1, 2 * D)
    scatter.tick(13)
    passed = [remote(ref.at[at.c], ref.at[at.c], xs.at[5 + q], xr.at[5 + q], at.to_c) for q, ref in enumerate((dall, lall))]
    landed = [remote(ref.at[1 - at.c], ref.at[1 - at.c], xs.at[5 + q], xr.at[5 + q], at.to_c) for q, ref in enumerate((dall, lall))]
    passed[0].wait_send()
    landed[0].wait_recv()

    def latents(ref, first, count):
        total = jnp.zeros((n, 32), f32)
        for q in range(count):
            cols = slice(q * 512, (q + 1) * 512)
            x = jnp.concatenate([ref[k, :, :, cols].reshape(n // 2, 1, 512) for k in range(2)], axis=1).reshape(n, 512)
            dsum[:, (first + q) * 512 : (first + q + 1) * 512] = jnp.sum(x, axis=0, keepdims=True)
            total += ada_columns(x.astype(bf), first + q)
        return total

    total = latents(dall, 4, 8)
    each_mate(n, me, lambda k, to, fr: remote(lsrc, lall.at[at.c, fr // 2], s6.at[k], r6.at[k], to).wait())
    passed[1].start()
    scatter.tick(14)
    passed[1].wait_send()
    landed[1].wait_recv()
    total += latents(lall, 0, 4)
    csrc[:, :, 0:32] = total.reshape(n, 1, 32)
    each_peer(n, me, lambda k, to, fr: remote(csrc.at[to], crec.at[me], s5.at[k], r5.at[k], to).start())
    crec[pl.ds(me, 1)] = csrc[pl.ds(me, 1)]
    each_peer(n, me, lambda k, to, fr: remote(esrc.at[to], erec.at[fr], s4.at[k], r4.at[k], to).wait())
    bsum[...] = jnp.sum(erec[...], axis=0)
    scatter.tick(15)
    each_peer(n, me, lambda k, to, fr: remote(csrc.at[to], crec.at[fr], s5.at[k], r5.at[k], to).wait())
    scatter.tick(16)
    done.wait()
    scatter.finish()
    gather.finish()


def block(n, *a):
    dma = pltpu.SemaphoreType.DMA
    regular = pltpu.SemaphoreType.REGULAR
    vm = pltpu.VMEM
    return pl.pallas_call(
        functools.partial(block_kernel, n),
        out_shape=(sd((S, D), bf), sd((S, D), f32), sd((32, 18 * D), f32), sd((1, 512), f32), sd((1, 6 * D), f32), sd((n, 1, 128), f32))
        + (sd((12, 4, 2, 2, 2, 32, 1024), bf), sd((NJ, 2, 2, 2, 2, 32, 1024), f32), sd((4, S, 768), bf), sd((4, S, 256), bf)),
        in_specs=[V] * 3 + [A],
        out_specs=[A] * 2 + [V] * 4 + [A] * 4,
        scratch_shapes=[vm((12, 32, 1024), bf), vm((2, 32, 6 * D), bf), vm((n // 2, 2, 16, 128), bf), vm((n, 32), bf)]
        + [vm((n // 2, 1, 6 * D), f32), vm((1, 4 * D), f32), vm((2, n // 2, 1, 4 * D), f32), vm((1, 2 * D), f32), vm((2, n // 2, 1, 2 * D), f32), vm((n, 1, 512), f32), vm((n, 1, 512), f32), vm((n, 1, 128), f32)]
        + [vm((6, 1, D), f32), vm((2, 1, D), f32), vm((4, 1, 768), f32), vm((NJ, 1, CH), f32), vm((6, 1, D), f32), vm((2, 1, D), f32), vm((NJ, 1, CH), f32), vm((4, 1, 512), f32)]
        + [vm((16, 2, 32, S), bf), vm((16, 2, 32, S), bf), vm((4, 4, S), f32), vm((S, D), bf), vm((S, D), f32)]
        + [vm((2, S, 1024), bf), vm((2, S, 1024), bf), vm((2, 16, 32, S), bf)]
        + [dma((n,))] * 2
        + [dma((2, n))] * 2
        + [dma((n,))] * 8
        + [dma((7,)), dma((7,)), dma((2, 3)), dma((2, 3)), regular, regular]
        + [dma((2,)), dma((2,)), dma((5,)), dma((2,))]
        + gather_sems(12)
        + Scatter.shapes,
        compiler_params=pltpu.CompilerParams(collective_id=0, has_side_effects=True, vmem_limit_bytes=VMEM_BYTES),
        name="block",
    )(*a)


def adam_step(param, grad, first, second, decay):
    new_first = beta_first * first + (1.0 - beta_first) * grad
    new_second = beta_second * second + (1.0 - beta_second) * grad * grad
    step_size = learn_rate / (1.0 - beta_first**STEP)
    denom = jnp.sqrt(new_second / (1.0 - beta_second**STEP)) + adam_eps
    new_param = param - step_size * new_first / denom - learn_rate * decay * param
    return (new_param, new_first, new_second)


def plain(n, tok, gout, condition, weights, biases):
    me = lax.axis_index("dp")
    rows = D // n
    wb = weights.astype(bf)
    qkvo = wb[:, : 4 * D].reshape(rows, 4, 4, 256).transpose(2, 0, 1, 3).reshape(4, rows, 1024)
    updn = wb[:, 4 * D : 4 * D + 2 * FF].reshape(rows, 2, NJ, CH).transpose(2, 0, 1, 3).reshape(NJ, rows, 1024)
    mine = jnp.concatenate([qkvo, updn], axis=0)
    ada_l = wb[:, 4 * D + 2 * FF :]
    cond_act = jax.nn.silu(condition).astype(bf)
    bias_full = lax.all_gather(biases.astype(bf), "dp", axis=0, tiled=True).astype(f32)
    cond_all = lax.all_gather(cond_act, "dp", axis=0, tiled=True)
    cond_cols = lax.dynamic_slice_in_dim(cond_all, me * rows, rows, 1)
    mod = lax.psum_scatter(jnp.dot(cond_cols, ada_l, preferred_element_type=f32), "dp", scatter_dimension=0, tiled=True)
    mod = jnp.concatenate([(mod[0] + bias_full[4 * D + FF :]).reshape(6, D), jnp.zeros((2, D), f32)], axis=0)
    zrow = jnp.zeros((D,), f32)
    bqkv = jnp.stack([bias_full[:D], zrow, bias_full[D : 2 * D]]).reshape(3, 4, 256).transpose(1, 0, 2).reshape(4, 1, 768)
    brows = jnp.stack([zrow, zrow, bias_full[2 * D : 3 * D], bias_full[3 * D + FF : 4 * D + FF], zrow, zrow, zrow, zrow])
    bup = bias_full[3 * D : 3 * D + FF].reshape(NJ, 1, CH)
    wall = lax.all_gather(mine, "dp", axis=1, tiled=True)
    qkv, attn_t, lse, h1t = ka(tok, mod, bqkv, wall)
    bo, dx1, dat, dw_mlp, dw_out, dmod_b, db, db_up = kb(512, tok, gout, attn_t, mod, brows, bup, wall)
    ig, dw_qkv, dmod_a, db_qkv = kc(1024, tok, mod, qkv, dat, lse, dx1, h1t, wall)
    g_mlp = lax.psum_scatter(dw_mlp, "dp", scatter_dimension=2, tiled=True)
    g_out = lax.psum_scatter(dw_out, "dp", scatter_dimension=0, tiled=True)
    g_qkv = lax.psum_scatter(dw_qkv, "dp", scatter_dimension=1, tiled=True)
    g_qkv = g_qkv.reshape(4, rows, 3, 256).transpose(1, 2, 0, 3).reshape(rows, 3 * D)
    g_mlp = g_mlp.transpose(2, 1, 0, 3).reshape(rows, 2 * FF)
    dmod = (dmod_a + dmod_b)[:6].reshape(1, 6 * D)
    db_qkv = db_qkv.reshape(4, 3, 256).transpose(1, 0, 2).reshape(3, D)
    bias_row = jnp.concatenate([db_qkv[0], db_qkv[2], db[2], db_up.reshape(FF), db[3], dmod[0]])
    bias_grad = lax.psum_scatter(bias_row, "dp", scatter_dimension=0, tiled=True)
    dmod_all = lax.all_gather(dmod.astype(bf), "dp", axis=0, tiled=True)
    g_ada = lax.dot_general(cond_cols, dmod_all, TN, preferred_element_type=f32)
    cond_part = lax.dot_general(dmod_all, ada_l, NT, preferred_element_type=f32)
    cond_grad = lax.all_to_all(cond_part, "dp", split_axis=0, concat_axis=1, tiled=True)
    return bo, ig, cond_grad, jnp.concatenate([g_qkv, g_out, g_mlp, g_ada], axis=1), bias_grad


def finish_kernel(gw, w, m, v, bo, ig, gw_o, w_o, m_o, v_o, bo_o, ig_o):
    grad = gw[...]
    gw_o[...] = grad
    w_o[...], m_o[...], v_o[...] = adam_step(w[...], grad, m[...], v[...], weight_decay)
    bo_o[...] = bo[...]
    ig_o[...] = ig[...]


def finish(steps, *a):
    cols = pl.BlockSpec((32, 18 * D // steps), lambda i: (0, i))
    toks = pl.BlockSpec((S // steps, D), lambda i: (i, 0))
    specs = [cols] * 4 + [toks] * 2
    return pl.pallas_call(
        finish_kernel,
        grid=(steps,),
        out_shape=(sd((32, 18 * D), f32),) * 4 + (sd((S, D), bf), sd((S, D), f32)),
        in_specs=specs,
        out_specs=specs,
        compiler_params=pltpu.CompilerParams(vmem_limit_bytes=VMEM_BYTES),
        name="finish",
    )(*a)


def on_chips(n, tok, gout, condition, weights, biases):
    cond_act = jax.nn.silu(condition).reshape(8, 128)
    padded = jnp.pad(biases.reshape(7, 64), ((0, 1), (0, 64)))
    bo, ig, weight_grad, bsum, dsum, crec = block(n, tok, gout, jnp.concatenate([cond_act, padded]).astype(bf), weights)[:6]
    own = biases.shape[0]
    flat = jnp.concatenate([jnp.zeros((4 * D + FF,), f32), dsum[0]])
    bias_grad = bsum[0, :own] + lax.dynamic_slice_in_dim(flat, lax.axis_index("dp") * own, own, 0)
    return bo, ig, crec[:, 0, :32].reshape(1, D), weight_grad, bias_grad


def on_device(n, block_in, condition, out_grad, weights, biases, first_moment, second_moment, bias_first, bias_second):
    run = on_chips if n == 32 else plain
    bo, ig, cond_grad, weight_grad, bias_grad = run(n, block_in[0], out_grad[0], condition, weights, biases)
    sigma = jax.nn.sigmoid(condition)
    cond_grad = cond_grad * (sigma * (1.0 + condition * (1.0 - sigma)))
    if n == 32:
        weight_grad, new_weights, new_first, new_second, bo, ig = finish(STEPS, weight_grad, weights, first_moment, second_moment, bo, ig)
    else:
        new_weights, new_first, new_second = adam_step(weights, weight_grad, first_moment, second_moment, weight_decay)
    new_biases, new_bias_first, new_bias_second = adam_step(biases, bias_grad, bias_first, bias_second, 0.0)
    return (bo[None], ig[None], cond_grad, weight_grad, bias_grad, new_weights, new_biases, new_first, new_second, new_bias_first, new_bias_second)


def solution(mesh):
    three, two, one = P("dp", None, None), P("dp", None), P("dp")
    return jax.shard_map(
        functools.partial(on_device, mesh.shape["dp"]),
        mesh=mesh,
        in_specs=(three, two, three, two, one, two, two, one, one),
        out_specs=(three, three, two, two, one, two, one, two, two, one, one),
        check_vma=False,
    )
```

profile of v0, /device:TPU:0, one launch (start us, length us, event | category | flops | bytes accessed | tf_op | source)
XLA Modules:
  0.0 331.9 jit_solution(8129496799655095368)
XLA Ops:
  0.6 1.3 convert_reduce_fusion
  1.9 0.7 convert.11
  2.6 0.1 reshape.31
  2.7 0.6 fusion.1.small
  3.3 311.3 %block.1 = (bf16[1024,1024]{1,0:T(8,128)(2,1)}, f32[1024,1024]{1,0:T(8,128)}, f32[32,18432]{1,0:T(8,128)}, f32[1,512]{1,0:T(1,128)}, f32[1,6144]{1,0:T(1,128)}, ...) custom-call(bf16[1024,1024]{1,0:T(8,128)(2,1)} %bitcast.8, ...), custom_call_target="tpu_custom_call" | custom-call | tf_op jit(solution)/shard_map/block/pallas_call | solution.py:1152
  314.6 13.5 %finish.1 = (f32[32,18432]{1,0:T(8,128)}, f32[32,18432]{1,0:T(8,128)}, f32[32,18432]{1,0:T(8,128)}, f32[32,18432]{1,0:T(8,128)}, bf16[1024,1024]{1,0:T(8,128)(2,1)}, /*index=5*/f32[1024,1024]{1,0:T(8,128)}) custom-call(f32[32,18432]{1,0:T(8,128)} %get-tuple-element.23.gw, f32[32,18432]{1,0:T(8,128)} %w.1, f32[32,18432]{1,0:T(8,128)} %m.1, f32[32,18432]{1,0:T(8,128)} %v.1, ...), custom_call_target="tpu_custom_call" | custom-call | tf_op jit(solution)/shard_map/finish/pallas_call | solution.py:1234
  328.2 1.4 multiply_subtract_fusion
  329.6 0.8 slice_reduce_fusion
  330.3 0.1 reshape_squeeze.3
  330.4 1.3 multiply_multiply_fusion
where the time goes:
time: 338 us; the launch traced here: 332 us
  Pallas kernels  325 us (96%)
  other arithmetic  5.3 us (2%)
    pallas_call x1, Pallas kernels, block(): pl.pallas_call(functools.partial(block_kernel, n), out_shape=(sd((S, D),...  311 us
    pallas_call x1, Pallas kernels, finish(): pl.pallas_call(finish_kernel, grid=(steps,), out_shape=(sd((32, 18 * D),...  13.5 us

commit v1 on v0

--- a/solution.py
+++ b/solution.py
@@ -14,7 +14,7 @@
 CH = 512
 NJ = FF // CH
 VMEM_BYTES = 64 * 2**20
-STEPS = 8
+STEPS = 4
 learn_rate = 0.01
 beta_first = 0.9
 beta_second = 0.95
@@ -774,6 +774,8 @@
                 kp = qkv[slot, :, p * 384 + 128 : p * 384 + 256]
                 vT = qkv[slot, :, p * 384 + 256 : p * 384 + 384].T
                 q = qkv[slot, :, p * 384 : p * 384 + 128]
+                if p == 1:
+                    gather.tick(5 + g, (3,))
                 scores = [dot(lane_half(kp, h), q, NT) for h in range(2)]
                 probs = []
                 for h in range(2):
@@ -785,7 +787,7 @@
                 for h in range(2):
                     o = dot(vT[h * 64 : (h + 1) * 64], probs[h])
                     attnT[pl.ds(g * 4 + p * 2 + h, 1)] = o.astype(bf).reshape(1, 2, 32, S)
-            gather.tick(5 + g)
+            gather.tick(5 + g, (5, 4, 2, 1))
             when(g < 3, lambda: fetch(g + 1, wbuf, 1 - slot).start())
             return 0
 

time: 338 us -> 336 us (level)
  no operation moved by 1% of the time
where the time goes in v1:
time: 336 us; the launch traced here: 330 us
  Pallas kernels  323 us (96%)
  other arithmetic  5.29 us (2%)
    pallas_call x1, Pallas kernels, block(): pl.pallas_call(functools.partial(block_kernel, n), out_shape=(sd((S, D),...  311 us
    pallas_call x1, Pallas kernels, finish(): pl.pallas_call(finish_kernel, grid=(steps,), out_shape=(sd((32, 18 * D),...  11.6 us

profile of v1, /device:TPU:0, one launch (start us, length us, event | category | flops | bytes accessed | tf_op | source)
XLA Modules:
  0.0 329.8 jit_solution(14465306028532918850)
XLA Ops:
  0.6 1.3 convert_reduce_fusion
  1.9 0.7 convert.11
  2.6 0.1 reshape.31
  2.7 0.6 fusion.1.small
  3.3 311.1 %block.1 = (bf16[1024,1024]{1,0:T(8,128)(2,1)}, f32[1024,1024]{1,0:T(8,128)}, f32[32,18432]{1,0:T(8,128)}, f32[1,512]{1,0:T(1,128)}, f32[1,6144]{1,0:T(1,128)}, ...) custom-call(bf16[1024,1024]{1,0:T(8,128)(2,1)} %bitcast.8, ...), custom_call_target="tpu_custom_call" | custom-call | tf_op jit(solution)/shard_map/block/pallas_call | solution.py:1154
  314.4 11.6 %finish.1 = (f32[32,18432]{1,0:T(8,128)}, f32[32,18432]{1,0:T(8,128)}, f32[32,18432]{1,0:T(8,128)}, f32[32,18432]{1,0:T(8,128)}, bf16[1024,1024]{1,0:T(8,128)(2,1)}, /*index=5*/f32[1024,1024]{1,0:T(8,128)}) custom-call(f32[32,18432]{1,0:T(8,128)} %get-tuple-element.23.gw, f32[32,18432]{1,0:T(8,128)} %w.1, f32[32,18432]{1,0:T(8,128)} %m.1, f32[32,18432]{1,0:T(8,128)} %v.1, ...), custom_call_target="tpu_custom_call" | custom-call | tf_op jit(solution)/shard_map/finish/pallas_call | solution.py:1236
  326.0 1.4 multiply_subtract_fusion
  327.4 0.8 slice_reduce_fusion
  328.2 0.1 reshape_squeeze.3
  328.2 1.3 multiply_multiply_fusion
